TPU v7x, 32 devices: a whole 2x2x4 slice. The times are simulated.
32 devices in a mesh: seq: 16 (over z, y, core), head: 2 (over x).
Axes of the slice: x: 2, y: 2, z: 4, core: 2. Of those that a mesh axis runs over, the one named last changes fastest.
Arguments:
- queries: bfloat16 [4096, 8192], P(('seq', 'head')), may hold values from -6 to 6
- keys: bfloat16 [4096, 8192], P(('seq', 'head')), may hold values from -6 to 6
- values: bfloat16 [4096, 8192], P(('seq', 'head')), may hold values from -70 to 70
- log_decay: float32 [64, 4096], P('head', 'seq'), may hold values from -1 to 0
- doc_lengths: int32 [32], replicated, may hold values from 1 to 1024, 4096 in all
- gain: float32 [8192], P('head'), may hold values from 0.25 to 1.75
Outputs:
- attended: bfloat16 [4096, 8192], P(('seq', 'head'))
All inputs are finite; a program needn't handle non-finite values.
Results may differ from a plain program's by a relative error of at most 0.001.
Values may be sent and summed in bfloat16 or wider, within the bound.
A program may use at most 128 MiB of HBM per device.

v0:
```python
import jax
import jax.numpy as jnp
from jax import lax
from jax.sharding import PartitionSpec as P

HIGHEST = lax.Precision.HIGHEST


def prefix(part, axis, combine, identity):
    place = lax.axis_index(axis)
    gathered = jax.tree.map(lambda a: lax.all_gather(a, axis), part)
    state = jax.tree.map(lambda a, e: jnp.zeros_like(a) + jnp.asarray(e, a.dtype), part, identity)

    def one(turn, state):
        return combine(
            state, jax.tree.map(lambda a: lax.dynamic_index_in_dim(a, turn, 0, False), gathered)
        )

    return lax.fori_loop(0, place, one, state)


def link(earlier, later):
    factor_one, state_one = earlier
    factor_two, state_two = later
    return (factor_one * factor_two, factor_two[:, None, None] * state_one + state_two)


def make_identity(amount, head_width):
    return (
        jnp.ones((amount,), jnp.float32),
        jnp.zeros((amount, head_width, head_width), jnp.float32),
    )


def local(queries, keys, values, log_decay, doc_lengths, gain):
    query_rows, key_rows, value_rows = (
        lax.all_to_all(queries, "head", split_axis=1, concat_axis=0, tiled=True),
        lax.all_to_all(keys, "head", split_axis=1, concat_axis=0, tiled=True),
        lax.all_to_all(values, "head", split_axis=1, concat_axis=0, tiled=True),
    )
    head_count = log_decay.shape[0]
    row_count = key_rows.shape[0]
    head_width = key_rows.shape[1] // head_count
    doc_ends = jnp.cumsum(doc_lengths)
    first_row = lax.axis_index("seq") * row_count
    positions = first_row + jnp.arange(row_count, dtype=jnp.int32)
    doc_ids = jnp.sum((doc_ends[None, :] <= positions[:, None]).astype(jnp.int32), axis=1)
    prior_doc = jnp.sum((doc_ends <= first_row - 1).astype(jnp.int32))
    order_ids = jnp.arange(row_count, dtype=jnp.int32)
    allowed = (order_ids[:, None] >= order_ids[None, :]) & (doc_ids[:, None] == doc_ids[None, :])
    decay_sum = jnp.cumsum(log_decay, axis=1)
    tailing = (
        jnp.exp(decay_sum[:, -1:] - decay_sum)
        * (doc_ids == doc_ids[-1]).astype(jnp.float32)[None, :]
    )
    leading = jnp.exp(decay_sum) * (doc_ids == prior_doc).astype(jnp.float32)[None, :]
    carried = jnp.exp(decay_sum[:, -1]) * (doc_ids[-1] == prior_doc).astype(jnp.float32)
    head_ids = jnp.arange(head_count, dtype=jnp.int32)

    def pick(block, head_index):
        return lax.dynamic_slice_in_dim(block, head_index * head_width, head_width, 1)

    def own_state(head_index):
        weighted = pick(key_rows, head_index).astype(jnp.float32) * tailing[head_index][:, None]
        value_part = pick(value_rows, head_index).astype(jnp.float32)
        return jnp.einsum(
            "jd,je->de", weighted, value_part, precision=HIGHEST, preferred_element_type=jnp.float32
        )

    def within(head_index):
        scores = lax.dot_general(
            pick(query_rows, head_index),
            pick(key_rows, head_index),
            (((1,), (1,)), ((), ())),
            preferred_element_type=jnp.float32,
        )
        gaps = decay_sum[head_index][:, None] - decay_sum[head_index][None, :]
        weights = jnp.where(allowed, jnp.exp(jnp.where(allowed, gaps, 0.0)), 0.0)
        value_part = pick(value_rows, head_index).astype(jnp.float32)
        return jnp.dot(
            scores * weights, value_part, precision=HIGHEST, preferred_element_type=jnp.float32
        )

    def across(paired):
        head_index, state = paired
        scaled = pick(query_rows, head_index).astype(jnp.float32) * leading[head_index][:, None]
        return jnp.dot(scaled, state, precision=HIGHEST, preferred_element_type=jnp.float32)

    own = lax.map(own_state, head_ids)
    total_factor, incoming = prefix(
        (carried, own), "seq", link, make_identity(head_count, head_width)
    )
    far = lax.map(across, (head_ids, incoming))
    near = lax.map(within, head_ids)
    mixed = near + far
    mean_square = jnp.mean(mixed * mixed, axis=-1, keepdims=True)
    normed = mixed * lax.rsqrt(mean_square + 1e-06) * gain.reshape(head_count, 1, head_width)
    merged = (
        jnp.transpose(normed, (1, 0, 2))
        .reshape(row_count, head_count * head_width)
        .astype(jnp.bfloat16)
    )
    return lax.all_to_all(merged, "head", split_axis=0, concat_axis=1, tiled=True)


def solution(mesh):
    return jax.shard_map(
        local,
        mesh=mesh,
        in_specs=(
            P(("seq", "head"), None),
            P(("seq", "head"), None),
            P(("seq", "head"), None),
            P("head", "seq"),
            P(),
            P("head"),
        ),
        out_specs=P(("seq", "head"), None),
        check_vma=False,
    )
```

profile of v0, /device:TPU:29, one launch (start us, length us, event | category | flops | bytes accessed | tf_op | source)
XLA Modules:
  0.0 685.4 jit_solution(13325891742446281327)
XLA Ops:
  6.5 3.1 copy.61
  9.7 3.9 all-to-all-start.1
  16.6 3.2 copy.60
  19.8 18.0 %all-to-all-done.1 = bf16[128,2,4096]{2,0,1:T(8,128)(2,1)S(1)} async-done(((bf16[128,2,4096]{2,0,1:T(8,128)(2,1)}), bf16[128,2,4096]{2,0,1:T(8,128)(2,1)S(1)}, u32[]{:S(2)}, u32[]{:S(2)}) %all-to-all-start.1) | async-done | bytes 2097184 | tf_op jit(solution)/shard_map/all_to_all | solution.py:38
  39.1 3.8 all-to-all-start.2
  45.4 20.7 %all-to-all-done.2 = bf16[128,2,4096]{2,0,1:T(8,128)(2,1)S(1)} async-done(((bf16[128,2,4096]{2,0,1:T(8,128)(2,1)}), bf16[128,2,4096]{2,0,1:T(8,128)(2,1)S(1)}, u32[]{:S(2)}, u32[]{:S(2)}) %all-to-all-start.2) | async-done | bytes 2097184 | tf_op jit(solution)/shard_map/all_to_all | solution.py:39
  67.7 142.4 %while.43 = (s32[]{:T(128)}, f32[32,128,128]{2,1,0:T(8,128)S(1)}, s32[32]{0:T(128)S(1)}, bf16[256,4096]{1,0:T(8,128)(2,1)}, f32[32,256]{1,0:T(8,128)S(1)}, /*ind...) while((s32[]{:T(128)}, f32[32,128,128]{2,1,0:T(8,128)S(1)}, ...), condition=%wide.region_8.9_spmd, body=%wide.region_7.8_spmd.sunk | while | flops 50397192 | bytes 201421 | solution.py:89
  211.5 3.1 copy.62
  214.7 3.9 all-to-all-start
  220.2 29.7 %all-reduce = f32[512]{0:T(512)S(1)} all-reduce(f32[512]{0:T(512)S(1)} %dynamic-update-slice), channel_id=2, replica_groups=mesh['seq'=16,'head'=2] {'seq'}, use_global_device_ids=true, to_apply=%add | all-reduce | flops 512 | bytes 4096
  249.9 2.5 broadcast.44.clone
  252.4 192.6 %while.46 = (s32[]{:T(128)}, f32[32,256,128]{2,1,0:T(8,128)}, s32[32]{0:T(128)S(1)}, bf16[256,4096]{1,0:T(8,128)(2,1)S(1)}, bf16[256,4096]{1,0:T(8,128)(2,1)}, /...) while((s32[]{:T(128)}, f32[32,256,128]{2,1,0:T(8,128)}, ...), condition=%wide.region_5.6_spmd.clone, body=%wide.region_4.5_spmd.clone.sunk | while | flops 117899272 | bytes 859873 | solution.py:94
  446.6 30.4 %while.44 = (s32[]{:T(128)}, f32[32,128,128]{2,1,0:T(8,128)S(1)}, s32[]{:T(128)}, f32[16,32]{1,0:T(8,128)S(1)}, f32[16,32,128,128]{3,2,1,0:T(8,128)}, /*index=5*/s32[]{:T(128)}, s32[]{:T(128)}, s32[]{:T(128)}) while((s32[]{:T(128)}, f32[32,128,128]{2,1,0:T(8,128)S(1)}, s32[]{:T(128)}, f32[16,32]{1,0:T(8,128)S(1)}, ...), condition=%wide.region_10.11_spmd, body=%wide.region_9.10_spmd.sunk | while | flops 1048581 | bytes 6291967 | solution.py:19
  446.6 2.0 bitcast_add_fusion.2
  448.7 2.0 bitcast_add_fusion.2
  456.8 2.0 bitcast_add_fusion.2
  468.9 2.0 bitcast_add_fusion.2
  477.0 2.4 broadcast.44.clone.1
  479.4 157.6 %while.45 = (s32[]{:T(128)}, f32[32,256,128]{2,1,0:T(8,128)}, s32[32]{0:T(128)S(1)}, bf16[256,4096]{1,0:T(8,128)(2,1)}, f32[32,256]{1,0:T(8,128)S(1)}, /*index=5...) while((s32[]{:T(128)}, f32[32,256,128]{2,1,0:T(8,128)}, ...), condition=%wide.region_12.13_spmd, body=%wide.region_11.12_spmd.sunk | while | flops 50397192 | bytes 266449 | solution.py:93
  637.0 4.6 multiply_reduce_fusion
  644.5 2.3 convert_element_type.48
  646.7 25.3 %all_to_all.73 = bf16[2,128,4096]{2,1,0:T(8,128)(2,1)S(1)} all-to-all(bf16[2,128,4096]{2,1,0:T(8,128)(2,1)} %convert_element_type.48), channel_id=1, replica_groups=mesh['seq'=16,'head'=2] {'head'}, dimensions={0} | all-to-all | bytes 4194304 | tf_op jit(solution)/shard_map/all_to_all | solution.py:103
  672.0 2.5 copy.44
  674.5 4.1 copy.45
  (396 shorter events, 280.3 us)
Async XLA Ops:
  6.5 36.4 %copy-start = (f32[32,256]{1,0:T(8,128)S(1)}, f32[32,256]{1,0:T(8,128)}, u32[]{:S(2)}) copy-start(f32[32,256]{1,0:T(8,128)} %param.17) | copy-start | bytes 98308
  9.7 3.9 copy-start.7
  9.7 28.1 %all-to-all-start.1 = ((bf16[128,2,4096]{2,0,1:T(8,128)(2,1)}), bf16[128,2,4096]{2,0,1:T(8,128)(2,1)S(1)}, u32[]{:S(2)}, u32[]{:S(2)}) async-start(bf16[128,2,4096]{2,0,1:T(8,128)(2,1)} %bitcast.69), calls=%async_computation.1 | async-start | bytes 4194304 | tf_op jit(solution)/shard_map/all_to_all | solution.py:38
  37.8 1.3 copy-start.4
  39.1 27.1 %all-to-all-start.2 = ((bf16[128,2,4096]{2,0,1:T(8,128)(2,1)}), bf16[128,2,4096]{2,0,1:T(8,128)(2,1)S(1)}, u32[]{:S(2)}, u32[]{:S(2)}) async-start(bf16[128,2,4096]{2,0,1:T(8,128)(2,1)} %bitcast.68), calls=%async_computation.2 | async-start | bytes 4194304 | tf_op jit(solution)/shard_map/all_to_all | solution.py:39
  42.9 402.2 %all-gather.4.cloned.1.call-start = ((), (), s32[]{:S(2)}) async-start(), calls=%async_computation.4 | async-start | bytes 35651584 | tf_op jit(solution)/shard_map/all_gather | solution.py:11
  66.2 1.3 copy-start.3
  210.1 1.4 copy-start.2
  214.7 3.9 copy-start.8
  214.7 35.3 %all-to-all-start = ((bf16[128,2,4096]{2,0,1:T(8,128)(2,1)}), bf16[128,2,4096]{2,0,1:T(8,128)(2,1)S(1)}, u32[]{:S(2)}, u32[]{:S(2)}) async-start(bf16[128,2,4096]{2,0,1:T(8,128)(2,1)} %bitcast.70), calls=%async_computation | async-start | bytes 4194304 | tf_op jit(solution)/shard_map/all_to_all | solution.py:37
  445.0 1.3 copy-start.5
  637.0 4.7 copy-start.6
  674.5 4.1 copy-start.1
Sparse Core Ops, SparseCore 0:
  211.6 169.7 all-gather.3
where the time goes:
time: 696 us; the launch traced here: 685 us
  loops' own time  248 us (36%)
  matrix products  187 us (27%)
  local copies, waits for them, and re-layouts  89.6 us (13%)
  blocking collectives  54.9 us (8%)
  other arithmetic  39 us (6%)
  waiting for transfers between devices  38.8 us (6%)
  between operations  15.6 us (2%)
  starting transfers between devices  11.6 us (2%)
    another operation x1, loops' own time, local(): own = lax.map(own_state, head_ids)  83.9 us
    another operation x1, loops' own time, local(): near = lax.map(within, head_ids)  83.6 us
    another operation x1, loops' own time, local(): far = lax.map(across, (head_ids, incoming))  80.4 us
    dot_general x32, matrix products, across(): jnp.dot(scaled, state, precision=HIGHEST, preferred_element_type=jnp.floa...  57.9 us
    dot_general x32, matrix products, within(): jnp.dot(scores * weights, value_part, precision=HIGHEST, preferred_elemen...  56.8 us
    dynamic_slice x96, local copies, waits for them, and re-layouts, local(): own = lax.map(own_state, head_ids)  56.4 us
    dot_general x32, matrix products, own_state(): jnp.einsum('jd,je->de', weighted, value_part, precision=HIGHEST, preferre...  39.5 us
    dot_general x32, matrix products, within(): lax.dot_general(pick(query_rows, head_index), pick(key_rows, head_index),...  33.3 us
  transfers between devices with their start and end apart: 4, of which 2 were waited for; matrix products, arithmetic and copies ran while one was open for 18% of the time, Pallas kernels for 0%

commit v1 on v0

--- a/solution.py
+++ b/solution.py
@@ -1,6 +1,10 @@
+import functools
+
 import jax
 import jax.numpy as jnp
 from jax import lax
+from jax.experimental import pallas as pl
+from jax.experimental.pallas import tpu as pltpu
 from jax.sharding import PartitionSpec as P
 
 HIGHEST = lax.Precision.HIGHEST
@@ -103,18 +107,351 @@
     return lax.all_to_all(merged, "head", split_axis=0, concat_axis=1, tiled=True)
 
 
+MESH = pl.DeviceIdType.MESH
+GROUP = 8
+SUBS = 2
+TOP = 32766.0
+FAR_BELOW = -1e30
+
+
+def other(number, turn):
+    out = 0
+    for bit in (1, 2, 4):
+        a, b = (number // bit) % 2, (turn // bit) % 2
+        out = out + bit * (a + b - 2 * a * b)
+    return out
+
+
+def halves(x):
+    high = x.astype(jnp.bfloat16)
+    return high, (x - high.astype(jnp.float32)).astype(jnp.bfloat16)
+
+
+def to_code(state):
+    scale = jnp.maximum(jnp.max(jnp.abs(state), axis=0, keepdims=True), 1e-30) * (1.0 / TOP)
+    code = jnp.round(state * (1.0 / scale)).astype(jnp.int32).astype(jnp.int16)
+    return code, scale
+
+
+def from_code(code):
+    return code.astype(jnp.int32).astype(jnp.float32)
+
+
+def slab_kernel(
+    slabs,
+    doc_ref, q_ref, k_ref, v_ref, ld_ref, gain_ref, o_ref,
+    ld_all, gain_all, cum_t, bias, near,
+    s_out, s_in, sm_out, sm_in, e_out, e_in, em_out, em_in, t_out, t_in,
+    s_ss, s_rs, sm_ss, sm_rs, e_ss, e_rs, em_ss, em_rs, t_ss, t_rs, x_ss, x_rs,
+):
+    seq, half = lax.axis_index("seq"), lax.axis_index("head")
+    block = seq * 2 + half
+    slab, me = block // GROUP, block % GROUP
+    rows, width = q_ref.shape[0], q_ref.shape[0]
+    part = ld_ref.shape[0]
+    count = 2 * part
+    per_owner = count // GROUP
+    per_sub = per_owner // SUBS
+
+    def place(other_slab, number):
+        b = other_slab * GROUP + number
+        return (b // 2, b % 2)
+
+    barrier = pltpu.get_barrier_semaphore()
+    for turn in range(1, GROUP):
+        pl.semaphore_signal(barrier, inc=1, device_id=place(slab, other(me, turn)), device_id_type=MESH)
+
+    @pl.when(slab > 0)
+    def _():
+        pl.semaphore_signal(barrier, inc=1, device_id=place(slab - 1, me), device_id_type=MESH)
+
+    @pl.when(slab < slabs - 1)
+    def _():
+        pl.semaphore_signal(barrier, inc=1, device_id=place(slab + 1, me), device_id_type=MESH)
+
+    neighbours = GROUP - 1 + jnp.where(slab > 0, 1, 0) + jnp.where(slab < slabs - 1, 1, 0)
+    pl.semaphore_wait(barrier, neighbours)
+
+    mine = pl.ds(pl.multiple_of(half * part, part), part)
+    swaps = [
+        pltpu.make_async_remote_copy(
+            src_ref=ld_ref.at[:, pl.ds(pl.multiple_of((1 - half) * rows, rows), rows)],
+            dst_ref=ld_all.at[mine], send_sem=x_ss.at[0], recv_sem=x_rs.at[0],
+            device_id=(seq, 1 - half), device_id_type=MESH),
+        pltpu.make_async_remote_copy(
+            src_ref=gain_ref, dst_ref=gain_all.at[mine], send_sem=x_ss.at[1], recv_sem=x_rs.at[1],
+            device_id=(seq, 1 - half), device_id_type=MESH),
+    ]
+    for swap in swaps:
+        swap.start()
+    ld_all[mine, :] = ld_ref[:, pl.ds(pl.multiple_of(half * rows, rows), rows)]
+    gain_all[mine, :] = gain_ref[...]
+
+    first = block * rows
+    down = lax.broadcasted_iota(jnp.int32, (rows, rows), 0)
+    along = lax.broadcasted_iota(jnp.int32, (rows, rows), 1)
+    doc_down = jnp.zeros((rows, rows), jnp.int32)
+    doc_along = jnp.zeros((rows, rows), jnp.int32)
+    prior = jnp.int32(0)
+    final = jnp.int32(0)
+    end = jnp.int32(0)
+    for n in range(doc_ref.shape[0]):
+        end = end + doc_ref[n]
+        doc_down = doc_down + (down + first >= end).astype(jnp.int32)
+        doc_along = doc_along + (along + first >= end).astype(jnp.int32)
+        prior = prior + (end <= first - 1).astype(jnp.int32)
+        final = final + (end <= first + rows - 1).astype(jnp.int32)
+    bias[...] = jnp.where((down >= along) & (doc_down == doc_along), 0.0, FAR_BELOW)
+    doc_few = doc_down[:, :per_owner]
+    in_last = (doc_few == final).astype(jnp.float32)
+    in_prior = (doc_few == prior).astype(jnp.float32)
+    passes = (jnp.full((1, per_owner), final, jnp.int32) == prior).astype(jnp.float32)
+
+    for swap in swaps:
+        swap.wait()
+    cum = jnp.dot(
+        ld_all[...], (down <= along).astype(jnp.float32),
+        precision=HIGHEST, preferred_element_type=jnp.float32,
+    )
+    turned = jnp.transpose(jnp.concatenate([cum, jnp.zeros((rows - count, rows), jnp.float32)], axis=0))
+    for g in range(GROUP):
+        cum_t[g] = turned[:, g * per_owner:(g + 1) * per_owner]
+
+    def columns(g, c):
+        return pl.ds(pl.multiple_of((g * per_owner + c) * width, width), width)
+
+    def make_state(g, sub, code_ref, meta_ref):
+        sums = cum_t[g]
+        last = sums[rows - 1:rows, :]
+        tail = jnp.exp(last - sums) * in_last
+        carry = jnp.exp(last) * passes
+        for i in range(per_sub):
+            c = sub * per_sub + i
+            cols = columns(g, c)
+            high, low = halves(k_ref[:, cols].astype(jnp.float32) * tail[:, c:c + 1])
+            value = v_ref[:, cols]
+            state = lax.dot_general(
+                jnp.concatenate([high, low], axis=0), jnp.concatenate([value, value], axis=0),
+                (((0,), (0,)), ((), ())), preferred_element_type=jnp.float32,
+            )
+            code, scale = to_code(state)
+            code_ref[i] = code
+            meta_ref[i:i + 1, :] = scale
+            meta_ref[per_sub + i:per_sub + i + 1, :] = jnp.broadcast_to(carry[:, c:c + 1], (1, width))
+
+    def send_pair(sub, turn, out, into, ss, rs, m_out, m_in, m_ss, m_rs, slot, peer):
+        to = place(slab, peer)
+        return [
+            pltpu.make_async_remote_copy(
+                src_ref=m_out.at[sub, slot], dst_ref=m_in.at[sub, me], send_sem=m_ss.at[sub, turn],
+                recv_sem=m_rs.at[sub, me], device_id=to, device_id_type=MESH),
+            pltpu.make_async_remote_copy(
+                src_ref=out.at[sub, slot], dst_ref=into.at[sub, me], send_sem=ss.at[sub, turn],
+                recv_sem=rs.at[sub, me], device_id=to, device_id_type=MESH),
+        ]
+
+    def state_pair(sub, turn):
+        return send_pair(sub, turn, s_out, s_in, s_ss, s_rs, sm_out, sm_in, sm_ss, sm_rs, turn, other(me, turn))
+
+    def prefix_pair(sub, turn):
+        peer = other(me, turn)
+        return send_pair(sub, turn, e_out, e_in, e_ss, e_rs, em_out, em_in, em_ss, em_rs, peer, peer)
+
+    def wait_arrival(sub, number, into, rs, m_in, m_rs):
+        for ref, sem in ((m_in, m_rs), (into, rs)):
+            pltpu.make_async_remote_copy(
+                src_ref=ref.at[sub, number], dst_ref=ref.at[sub, number], send_sem=sem.at[sub, number],
+                recv_sem=sem.at[sub, number], device_id=place(slab, number), device_id_type=MESH,
+            ).wait_recv()
+
+    def send_states(sub):
+        @pl.loop(0, GROUP - 1)
+        def _(step):
+            turn = GROUP - 1 - step
+            make_state(other(me, turn), sub, s_out.at[sub, turn], sm_out.at[sub, turn])
+            for copy in state_pair(sub, turn):
+                copy.start()
+
+        make_state(me, sub, s_in.at[sub, me], sm_in.at[sub, me])
+
+    def near_heads(low, high):
+        @pl.loop(low, high)
+        def _(g):
+            sums = cum_t[g]
+            for c in range(per_owner):
+                cols = columns(g, c)
+                scores = lax.dot_general(
+                    q_ref[:, cols], k_ref[:, cols], (((1,), (1,)), ((), ())),
+                    preferred_element_type=jnp.float32,
+                )
+                spread = jnp.broadcast_to(sums[:, c:c + 1], (rows, rows))
+                flat = cum_rows[pl.ds(g * per_owner + c, 1), :]
+                high_part, low_part = halves(scores * jnp.exp(spread - flat + bias[...]))
+                value = v_ref[:, cols]
+                near[:, cols] = jnp.dot(
+                    jnp.concatenate([high_part, low_part], axis=1),
+                    jnp.concatenate([value, value], axis=0),
+                    preferred_element_type=jnp.float32,
+                )
+
+    def slab_totals(sub):
+        @pl.loop(1, GROUP)
+        def _(turn):
+            wait_arrival(sub, other(me, turn), s_in, s_rs, sm_in, sm_rs)
+
+        @pl.when(slab < slabs - 1)
+        def _():
+            @pl.loop(0, per_sub)
+            def _(i):
+                state = jnp.zeros((width, width), jnp.float32)
+                for b in range(GROUP):
+                    state = state * sm_in[sub, b, pl.ds(per_sub + i, 1), :] + from_code(s_in[sub, b, i]) * sm_in[
+                        sub, b, pl.ds(i, 1), :]
+                t_out[sub, i] = state
+
+            total_copy(sub).start()
+
+    def total_copy(sub):
+        return pltpu.make_async_remote_copy(
+            src_ref=t_out.at[sub], dst_ref=t_in.at[sub], send_sem=t_ss.at[sub], recv_sem=t_rs.at[sub],
+            device_id=place(slab + 1, me), device_id_type=MESH)
+
+    def send_prefixes(sub):
+        @pl.when(slab > 0)
+        def _():
+            pltpu.make_async_remote_copy(
+                src_ref=t_in.at[sub], dst_ref=t_in.at[sub], send_sem=t_ss.at[sub], recv_sem=t_rs.at[sub],
+                device_id=place(slab - 1, me), device_id_type=MESH).wait_recv()
+
+        @pl.when(slab == 0)
+        def _():
+            t_in[sub] = jnp.zeros(t_in.shape[1:], jnp.float32)
+
+        @pl.loop(0, per_sub)
+        def _(i):
+            state = t_in[sub, i]
+            for b in range(GROUP):
+                code, scale = to_code(state)
+                e_out[sub, b, i] = code
+                em_out[sub, b, pl.ds(i, 1), :] = scale
+                if b < GROUP - 1:
+                    state = state * sm_in[sub, b, pl.ds(per_sub + i, 1), :] + from_code(s_in[sub, b, i]) * sm_in[
+                        sub, b, pl.ds(i, 1), :]
+
+        @pl.loop(0, GROUP - 1)
+        def _(step):
+            for copy in prefix_pair(sub, GROUP - 1 - step):
+                copy.start()
+
+    def finish(g, sub, codes, metas):
+        sums = cum_t[g]
+        lead = jnp.exp(sums) * in_prior
+        for i in range(per_sub):
+            c = sub * per_sub + i
+            cols = columns(g, c)
+            high, low = halves(from_code(codes[i]))
+            query = q_ref[:, cols]
+            far = jnp.dot(
+                jnp.concatenate([query, query], axis=1), jnp.concatenate([high, low], axis=0),
+                preferred_element_type=jnp.float32,
+            )
+            mixed = near[:, cols] + far * lead[:, c:c + 1] * metas[i:i + 1, :]
+            square = jnp.mean(mixed * mixed, axis=1, keepdims=True)
+            gains = gain_all[pl.ds(g * per_owner + c, 1), :]
+            o_ref[:, cols] = (mixed * lax.rsqrt(square + 1e-06) * gains).astype(jnp.bfloat16)
+
+    cum_rows = ld_all
+    ld_all[...] = cum
+
+    for sub in range(SUBS):
+        send_states(sub)
+    cuts = [0, GROUP // 2, 3 * GROUP // 4, GROUP]
+    near_heads(cuts[0], cuts[1])
+    slab_totals(0)
+    near_heads(cuts[1], cuts[2])
+    send_prefixes(0)
+    slab_totals(1)
+    near_heads(cuts[2], cuts[3])
+    send_prefixes(1)
+    for sub in range(SUBS):
+        finish(me, sub, e_out.at[sub, me], em_out.at[sub, me])
+
+        @pl.loop(1, GROUP)
+        def _(turn, sub=sub):
+            g = other(me, turn)
+            wait_arrival(sub, g, e_in, e_rs, em_in, em_rs)
+            finish(g, sub, e_in.at[sub, g], em_in.at[sub, g])
+
+    for sub in range(SUBS):
+        @pl.loop(1, GROUP)
+        def _(turn, sub=sub):
+            for copy in state_pair(sub, turn) + prefix_pair(sub, turn):
+                copy.wait_send()
+
+        @pl.when(slab < slabs - 1)
+        def _(sub=sub):
+            total_copy(sub).wait_send()
+
+
+def by_slabs(slabs, queries, keys, values, log_decay, doc_lengths, gain):
+    rows, columns = queries.shape
+    part = log_decay.shape[0]
+    count = 2 * part
+    per_sub = count // GROUP // SUBS
+    width = columns // count
+    codes = pltpu.VMEM((SUBS, GROUP, per_sub, width, width), jnp.int16)
+    metas = pltpu.VMEM((SUBS, GROUP, 2 * per_sub, width), jnp.float32)
+    totals = pltpu.VMEM((SUBS, per_sub, width, width), jnp.float32)
+    sems = pltpu.SemaphoreType.DMA
+    vmem = pl.BlockSpec(memory_space=pltpu.VMEM)
+    return pl.pallas_call(
+        functools.partial(slab_kernel, slabs),
+        out_shape=jax.ShapeDtypeStruct((rows, columns), jnp.bfloat16),
+        in_specs=[pl.BlockSpec(memory_space=pltpu.SMEM)] + [vmem] * 5,
+        out_specs=vmem,
+        scratch_shapes=[
+            pltpu.VMEM((count, rows), jnp.float32),
+            pltpu.VMEM((count, width), jnp.float32),
+            pltpu.VMEM((GROUP, rows, count // GROUP), jnp.float32),
+            pltpu.VMEM((rows, rows), jnp.float32),
+            pltpu.VMEM((rows, columns), jnp.float32),
+            codes, codes, metas, metas, codes, codes, metas, metas, totals, totals,
+        ] + [sems((SUBS, GROUP))] * 8 + [sems((SUBS,))] * 2 + [sems((2,))] * 2,
+        compiler_params=pltpu.CompilerParams(
+            collective_id=0, has_side_effects=True, vmem_limit_bytes=48 * 1024 * 1024
+        ),
+        cost_estimate=pl.CostEstimate(
+            flops=14 * count * rows * rows * width, bytes_accessed=8 * rows * columns,
+            transcendentals=count * rows * rows,
+        ),
+    )(doc_lengths, queries, keys, values, log_decay, gain.reshape(part, width))
+
+
 def solution(mesh):
-    return jax.shard_map(
-        local,
-        mesh=mesh,
-        in_specs=(
-            P(("seq", "head"), None),
-            P(("seq", "head"), None),
-            P(("seq", "head"), None),
-            P("head", "seq"),
-            P(),
-            P("head"),
-        ),
-        out_specs=P(("seq", "head"), None),
-        check_vma=False,
-    )
+    devices = mesh.shape["seq"] * mesh.shape["head"]
+
+    def run(queries, keys, values, log_decay, doc_lengths, gain):
+        rows = queries.shape[0] // devices
+        heads = log_decay.shape[0]
+        width = queries.shape[1] // heads
+        fits = (
+            mesh.shape["head"] == 2 and devices % GROUP == 0 and rows == width == 128
+            and GROUP * rows * 4 >= queries.shape[0] and heads % (GROUP * SUBS) == 0 and heads <= rows
+        )
+        body = functools.partial(by_slabs, devices // GROUP) if fits else local
+        return jax.shard_map(
+            body,
+            mesh=mesh,
+            in_specs=(
+                P(("seq", "head"), None),
+                P(("seq", "head"), None),
+                P(("seq", "head"), None),
+                P("head", "seq"),
+                P(),
+                P("head"),
+            ),
+            out_specs=P(("seq", "head"), None),
+            check_vma=False,
+        )(queries, keys, values, log_decay, doc_lengths, gain)
+
+    return run

time: 696 us -> 66.9 us (0.10)
  the two profiles are of different devices: /device:TPU:29 before, /device:TPU:0 now
where the time goes in v1:
time: 66.9 us; the launch traced here: 66.6 us
  Pallas kernels  61.6 us (92%)
  local copies, waits for them, and re-layouts  5.04 us (8%)
    pallas_call x1, Pallas kernels, by_slabs(): pl.pallas_call(functools.partial(slab_kernel, slabs), out_shape=jax.Shape...  61.6 us
    unnamed x9, local copies, waits for them, and re-layouts  5.04 us

profile of v1, /device:TPU:0, one launch (start us, length us, event | category | flops | bytes accessed | tf_op | source)
XLA Modules:
  0.0 66.6 jit_solution(3253615157439874260)
XLA Ops:
  0.0 0.0 copy-start
  0.0 1.6 %copy-done = bf16[128,8192]{1,0:T(8,128)(2,1)S(1)} copy-done((bf16[128,8192]{1,0:T(8,128)(2,1)S(1)}, bf16[128,8192]{1,0:T(8,128)(2,1)}, u32[]{:S(2)}) %copy-start) | copy-done | bytes 2097176
  1.6 0.0 copy-start.1
  1.6 0.8 %copy-done.1 = f32[32,256]{1,0:T(8,128)S(1)} copy-done((f32[32,256]{1,0:T(8,128)S(1)}, f32[32,256]{1,0:T(8,128)}, u32[]{:S(2)}) %copy-start.1) | copy-done | bytes 32792
  2.4 0.0 copy-start.2
  2.4 0.7 %copy-done.2 = f32[4096]{0:T(1024)S(1)} copy-done((f32[4096]{0:T(1024)S(1)}, f32[4096]{0:T(1024)}, u32[]{:S(2)}) %copy-start.2) | copy-done | bytes 16408
  3.1 0.0 copy-start.3
  3.1 0.7 copy-done.3
  3.7 61.6 %shard_map.64 = bf16[128,8192]{1,0:T(8,128)(2,1)S(1)} custom-call(s32[32]{0:T(128)S(1)} %copy-done.3, bf16[128,8192]{1,0:T(8,128)(2,1)S(1)} %copy-done, bf16[128,8192]{1,0:T(8,128)(2,1)} %k_ref.1, bf16[128,8192]{1,0:T(8,128)(2,1)} %v_ref.1, f32[32,256]{1,0:T(8,128)S(1)} %copy-done.1, f32[32,128]{1,0:T(8,128)S(1)} %bitcast.1), custom_call_target="tpu_custom_call" | custom-call | flops 1879048192 | bytes 8388608 | tf_op jit(solution)/shard_map/pallas_call | solution.py:407
  65.3 1.3 %copy.8 = bf16[128,8192]{1,0:T(8,128)(2,1)} copy(bf16[128,8192]{1,0:T(8,128)(2,1)S(1)} %shard_map.64) | data formatting | bytes 4194304
Async XLA Ops:
  0.0 1.6 %copy-start = (bf16[128,8192]{1,0:T(8,128)(2,1)S(1)}, bf16[128,8192]{1,0:T(8,128)(2,1)}, u32[]{:S(2)}) copy-start(bf16[128,8192]{1,0:T(8,128)(2,1)} %q_ref.1) | copy-start | bytes 6291460
  1.6 0.8 %copy-start.1 = (f32[32,256]{1,0:T(8,128)S(1)}, f32[32,256]{1,0:T(8,128)}, u32[]{:S(2)}) copy-start(f32[32,256]{1,0:T(8,128)} %ld_ref.1) | copy-start | bytes 98308
  2.4 0.7 %copy-start.2 = (f32[4096]{0:T(1024)S(1)}, f32[4096]{0:T(1024)}, u32[]{:S(2)}) copy-start(f32[4096]{0:T(1024)} %param.11) | copy-start | bytes 49156
  3.1 0.7 copy-start.3

commit v2 on v1

--- a/solution.py
+++ b/solution.py
@@ -112,6 +112,7 @@
 SUBS = 2
 TOP = 32766.0
 FAR_BELOW = -1e30
+ORDER = (7, 6, 1, 5, 4, 3, 2)
 
 
 def other(number, turn):
@@ -122,6 +123,13 @@
     return out
 
 
+def turn_at(step):
+    out = 0
+    for i, turn in enumerate(ORDER):
+        out = out + jnp.where(step == i, turn, 0)
+    return out
+
+
 def halves(x):
     high = x.astype(jnp.bfloat16)
     return high, (x - high.astype(jnp.float32)).astype(jnp.bfloat16)
@@ -139,10 +147,11 @@
 
 def slab_kernel(
     slabs,
-    doc_ref, q_ref, k_ref, v_ref, ld_ref, gain_ref, o_ref,
+    doc_ref, q_far, k_far, v_far, ld_ref, gain_ref, o_ref,
+    q_ref, k_ref, v_ref,
     ld_all, gain_all, cum_t, bias, near,
     s_out, s_in, sm_out, sm_in, e_out, e_in, em_out, em_in, t_out, t_in,
-    s_ss, s_rs, sm_ss, sm_rs, e_ss, e_rs, em_ss, em_rs, t_ss, t_rs, x_ss, x_rs,
+    s_ss, s_rs, sm_ss, sm_rs, e_ss, e_rs, em_ss, em_rs, t_ss, t_rs, x_ss, x_rs, l_s,
 ):
     seq, half = lax.axis_index("seq"), lax.axis_index("head")
     block = seq * 2 + half
@@ -156,6 +165,13 @@
     def place(other_slab, number):
         b = other_slab * GROUP + number
         return (b // 2, b % 2)
+
+    loads = [
+        pltpu.make_async_copy(far_ref, near_ref, l_s.at[i])
+        for i, (far_ref, near_ref) in enumerate(((k_far, k_ref), (v_far, v_ref), (q_far, q_ref)))
+    ]
+    for load in loads:
+        load.start()
 
     barrier = pltpu.get_barrier_semaphore()
     for turn in range(1, GROUP):
@@ -228,11 +244,11 @@
         for i in range(per_sub):
             c = sub * per_sub + i
             cols = columns(g, c)
-            high, low = halves(k_ref[:, cols].astype(jnp.float32) * tail[:, c:c + 1])
-            value = v_ref[:, cols]
-            state = lax.dot_general(
-                jnp.concatenate([high, low], axis=0), jnp.concatenate([value, value], axis=0),
-                (((0,), (0,)), ((), ())), preferred_element_type=jnp.float32,
+            high, low = halves(v_ref[:, cols].astype(jnp.float32) * tail[:, c:c + 1])
+            key = jnp.transpose(k_ref[:, cols])
+            state = jnp.dot(
+                jnp.concatenate([key, key], axis=1), jnp.concatenate([high, low], axis=0),
+                preferred_element_type=jnp.float32,
             )
             code, scale = to_code(state)
             code_ref[i] = code
@@ -267,7 +283,7 @@
     def send_states(sub):
         @pl.loop(0, GROUP - 1)
         def _(step):
-            turn = GROUP - 1 - step
+            turn = turn_at(step)
             make_state(other(me, turn), sub, s_out.at[sub, turn], sm_out.at[sub, turn])
             for copy in state_pair(sub, turn):
                 copy.start()
@@ -340,7 +356,7 @@
 
         @pl.loop(0, GROUP - 1)
         def _(step):
-            for copy in prefix_pair(sub, GROUP - 1 - step):
+            for copy in prefix_pair(sub, turn_at(step)):
                 copy.start()
 
     def finish(g, sub, codes, metas):
@@ -363,22 +379,25 @@
     cum_rows = ld_all
     ld_all[...] = cum
 
+    loads[0].wait()
+    loads[1].wait()
     for sub in range(SUBS):
         send_states(sub)
-    cuts = [0, GROUP // 2, 3 * GROUP // 4, GROUP]
-    near_heads(cuts[0], cuts[1])
+    loads[2].wait()
     slab_totals(0)
-    near_heads(cuts[1], cuts[2])
+    near_heads(0, 1)
     send_prefixes(0)
+    near_heads(1, 3)
     slab_totals(1)
-    near_heads(cuts[2], cuts[3])
+    near_heads(3, 4)
     send_prefixes(1)
+    near_heads(4, GROUP)
     for sub in range(SUBS):
         finish(me, sub, e_out.at[sub, me], em_out.at[sub, me])
 
-        @pl.loop(1, GROUP)
-        def _(turn, sub=sub):
-            g = other(me, turn)
+        @pl.loop(0, GROUP - 1)
+        def _(step, sub=sub):
+            g = other(me, turn_at(step))
             wait_arrival(sub, g, e_in, e_rs, em_in, em_rs)
             finish(g, sub, e_in.at[sub, g], em_in.at[sub, g])
 
@@ -407,18 +426,18 @@
     return pl.pallas_call(
         functools.partial(slab_kernel, slabs),
         out_shape=jax.ShapeDtypeStruct((rows, columns), jnp.bfloat16),
-        in_specs=[pl.BlockSpec(memory_space=pltpu.SMEM)] + [vmem] * 5,
+        in_specs=[pl.BlockSpec(memory_space=pltpu.SMEM)] + [pl.BlockSpec(memory_space=pltpu.HBM)] * 3 + [vmem] * 2,
         out_specs=vmem,
-        scratch_shapes=[
+        scratch_shapes=[pltpu.VMEM((rows, columns), jnp.bfloat16)] * 3 + [
             pltpu.VMEM((count, rows), jnp.float32),
             pltpu.VMEM((count, width), jnp.float32),
             pltpu.VMEM((GROUP, rows, count // GROUP), jnp.float32),
             pltpu.VMEM((rows, rows), jnp.float32),
             pltpu.VMEM((rows, columns), jnp.float32),
             codes, codes, metas, metas, codes, codes, metas, metas, totals, totals,
-        ] + [sems((SUBS, GROUP))] * 8 + [sems((SUBS,))] * 2 + [sems((2,))] * 2,
+        ] + [sems((SUBS, GROUP))] * 8 + [sems((SUBS,))] * 2 + [sems((2,))] * 2 + [sems((3,))],
         compiler_params=pltpu.CompilerParams(
-            collective_id=0, has_side_effects=True, vmem_limit_bytes=48 * 1024 * 1024
+            collective_id=0, has_side_effects=True, vmem_limit_bytes=56 * 1024 * 1024
         ),
         cost_estimate=pl.CostEstimate(
             flops=14 * count * rows * rows * width, bytes_accessed=8 * rows * columns,

time: 66.9 us -> 63.1 us (0.943)
  local copies, waits for them, and re-layouts: 5.04 us -> 3.1 us
  Pallas kernels: 61.6 us -> 59.8 us
    unnamed x9 -> x1, local copies, waits for them, and re-layouts: 5.04 us -> 3.1 us
    pallas_call x1, Pallas kernels: 61.6 us -> 59.8 us  [by_slabs(): pl.pallas_call(functools.partial(slab_kernel, slabs), out_shape=jax.Shape...]
where the time goes in v2:
time: 63.1 us; the launch traced here: 62.9 us
  Pallas kernels  59.8 us (95%)
  local copies, waits for them, and re-layouts  3.1 us (5%)
    pallas_call x1, Pallas kernels, by_slabs(): pl.pallas_call(functools.partial(slab_kernel, slabs), out_shape=jax.Shape...  59.8 us
    unnamed x1, local copies, waits for them, and re-layouts  3.1 us

profile of v2, /device:TPU:0, one launch (start us, length us, event | category | flops | bytes accessed | tf_op | source)
XLA Modules:
  0.0 62.9 jit_solution(16338851015495824622)
XLA Ops:
  0.0 59.8 %shard_map.64 = bf16[128,8192]{1,0:T(8,128)(2,1)} custom-call(s32[32]{0:T(128)} %doc_ref.1, bf16[128,8192]{1,0:T(8,128)(2,1)} %q_far.1, bf16[128,8192]{1,0:T(8,128)(2,1)} %k_far.1, bf16[128,8192]{1,0:T(8,128)(2,1)} %v_far.1, f32[32,256]{1,0:T(8,128)} %ld_ref.1, f32[32,128]{1,0:T(8,128)} %bitcast.1), custom_call_target="tpu_custom_call" | custom-call | flops 1879048192 | bytes 8388608 | tf_op jit(solution)/shard_map/pallas_call | solution.py:426
  59.8 3.1 %copy.8 = bf16[128,8192]{1,0:T(8,128)(2,1)} copy(bf16[128,8192]{1,0:T(8,128)(2,1)} %shard_map.64) | data formatting | bytes 4194304

commit v3 on v2

--- a/solution.py
+++ b/solution.py
@@ -110,6 +110,7 @@
 MESH = pl.DeviceIdType.MESH
 GROUP = 8
 SUBS = 2
+BATCH = 4
 TOP = 32766.0
 FAR_BELOW = -1e30
 ORDER = (7, 6, 1, 5, 4, 3, 2)
@@ -241,19 +242,21 @@
         last = sums[rows - 1:rows, :]
         tail = jnp.exp(last - sums) * in_last
         carry = jnp.exp(last) * passes
+        states = []
         for i in range(per_sub):
             c = sub * per_sub + i
             cols = columns(g, c)
             high, low = halves(v_ref[:, cols].astype(jnp.float32) * tail[:, c:c + 1])
             key = jnp.transpose(k_ref[:, cols])
-            state = jnp.dot(
+            states.append(jnp.dot(
                 jnp.concatenate([key, key], axis=1), jnp.concatenate([high, low], axis=0),
                 preferred_element_type=jnp.float32,
-            )
+            ))
+            meta_ref[per_sub + i:per_sub + i + 1, :] = jnp.broadcast_to(carry[:, c:c + 1], (1, width))
+        for i, state in enumerate(states):
             code, scale = to_code(state)
             code_ref[i] = code
             meta_ref[i:i + 1, :] = scale
-            meta_ref[per_sub + i:per_sub + i + 1, :] = jnp.broadcast_to(carry[:, c:c + 1], (1, width))
 
     def send_pair(sub, turn, out, into, ss, rs, m_out, m_in, m_ss, m_rs, slot, peer):
         to = place(slab, peer)
@@ -294,21 +297,33 @@
         @pl.loop(low, high)
         def _(g):
             sums = cum_t[g]
-            for c in range(per_owner):
-                cols = columns(g, c)
-                scores = lax.dot_general(
-                    q_ref[:, cols], k_ref[:, cols], (((1,), (1,)), ((), ())),
-                    preferred_element_type=jnp.float32,
-                )
-                spread = jnp.broadcast_to(sums[:, c:c + 1], (rows, rows))
-                flat = cum_rows[pl.ds(g * per_owner + c, 1), :]
-                high_part, low_part = halves(scores * jnp.exp(spread - flat + bias[...]))
-                value = v_ref[:, cols]
-                near[:, cols] = jnp.dot(
-                    jnp.concatenate([high_part, low_part], axis=1),
-                    jnp.concatenate([value, value], axis=0),
-                    preferred_element_type=jnp.float32,
-                )
+            for batch in range(0, per_owner, BATCH):
+                few = range(batch, batch + BATCH)
+                scores = [
+                    lax.dot_general(
+                        q_ref[:, columns(g, c)], k_ref[:, columns(g, c)], (((1,), (1,)), ((), ())),
+                        preferred_element_type=jnp.float32,
+                    )
+                    for c in few
+                ]
+                weights = [
+                    jnp.exp(
+                        jnp.broadcast_to(sums[:, c:c + 1], (rows, rows))
+                        - cum_rows[pl.ds(g * per_owner + c, 1), :] + bias[...]
+                    )
+                    for c in few
+                ]
+                parts = [halves(score * weight) for score, weight in zip(scores, weights)]
+                results = []
+                for c, (high_part, low_part) in zip(few, parts):
+                    value = v_ref[:, columns(g, c)]
+                    results.append(jnp.dot(
+                        jnp.concatenate([high_part, low_part], axis=1),
+                        jnp.concatenate([value, value], axis=0),
+                        preferred_element_type=jnp.float32,
+                    ))
+                for c, result in zip(few, results):
+                    near[:, columns(g, c)] = result
 
     def slab_totals(sub):
         @pl.loop(1, GROUP)
@@ -362,19 +377,24 @@
     def finish(g, sub, codes, metas):
         sums = cum_t[g]
         lead = jnp.exp(sums) * in_prior
+        fars = []
         for i in range(per_sub):
-            c = sub * per_sub + i
-            cols = columns(g, c)
             high, low = halves(from_code(codes[i]))
-            query = q_ref[:, cols]
-            far = jnp.dot(
+            query = q_ref[:, columns(g, sub * per_sub + i)]
+            fars.append(jnp.dot(
                 jnp.concatenate([query, query], axis=1), jnp.concatenate([high, low], axis=0),
                 preferred_element_type=jnp.float32,
-            )
-            mixed = near[:, cols] + far * lead[:, c:c + 1] * metas[i:i + 1, :]
-            square = jnp.mean(mixed * mixed, axis=1, keepdims=True)
+            ))
+        mixes, squares = [], []
+        for i, far in enumerate(fars):
+            c = sub * per_sub + i
+            mixed = near[:, columns(g, c)] + far * lead[:, c:c + 1] * metas[i:i + 1, :]
+            mixes.append(mixed)
+            squares.append(jnp.mean(mixed * mixed, axis=1, keepdims=True))
+        for i, (mixed, square) in enumerate(zip(mixes, squares)):
+            c = sub * per_sub + i
             gains = gain_all[pl.ds(g * per_owner + c, 1), :]
-            o_ref[:, cols] = (mixed * lax.rsqrt(square + 1e-06) * gains).astype(jnp.bfloat16)
+            o_ref[:, columns(g, c)] = (mixed * lax.rsqrt(square + 1e-06) * gains).astype(jnp.bfloat16)
 
     cum_rows = ld_all
     ld_all[...] = cum
@@ -437,7 +457,7 @@
             codes, codes, metas, metas, codes, codes, metas, metas, totals, totals,
         ] + [sems((SUBS, GROUP))] * 8 + [sems((SUBS,))] * 2 + [sems((2,))] * 2 + [sems((3,))],
         compiler_params=pltpu.CompilerParams(
-            collective_id=0, has_side_effects=True, vmem_limit_bytes=56 * 1024 * 1024
+            collective_id=0, has_side_effects=True, vmem_limit_bytes=40 * 1024 * 1024
         ),
         cost_estimate=pl.CostEstimate(
             flops=14 * count * rows * rows * width, bytes_accessed=8 * rows * columns,

time: 63.1 us -> 67.2 us (1.065)
  local copies, waits for them, and re-layouts: 3.1 us -> 8.22 us
  Pallas kernels: 59.8 us -> 58.6 us
    unnamed x1 -> x13, local copies, waits for them, and re-layouts: 3.1 us -> 8.22 us
    pallas_call x1, Pallas kernels: 59.8 us -> 58.6 us  [by_slabs(): pl.pallas_call(functools.partial(slab_kernel, slabs), out_shape=jax.Shape...]
where the time goes in v3:
time: 67.2 us; the launch traced here: 66.9 us
  Pallas kernels  58.6 us (87%)
  local copies, waits for them, and re-layouts  8.22 us (12%)
    pallas_call x1, Pallas kernels, by_slabs(): pl.pallas_call(functools.partial(slab_kernel, slabs), out_shape=jax.Shape...  58.6 us
    unnamed x13, local copies, waits for them, and re-layouts  8.22 us

profile of v3, /device:TPU:0, one launch (start us, length us, event | category | flops | bytes accessed | tf_op | source)
XLA Modules:
  0.0 66.9 jit_solution(16817480983626581509)
XLA Ops:
  0.0 0.0 copy-start
  0.0 1.6 %copy-done = bf16[128,8192]{1,0:T(8,128)(2,1)S(1)} copy-done((bf16[128,8192]{1,0:T(8,128)(2,1)S(1)}, bf16[128,8192]{1,0:T(8,128)(2,1)}, u32[]{:S(2)}) %copy-start) | copy-done | bytes 2097176
  1.6 0.0 copy-start.1
  1.6 1.6 %copy-done.1 = bf16[128,8192]{1,0:T(8,128)(2,1)S(1)} copy-done((bf16[128,8192]{1,0:T(8,128)(2,1)S(1)}, bf16[128,8192]{1,0:T(8,128)(2,1)}, u32[]{:S(2)}) %copy-start.1) | copy-done | bytes 2097176
  3.2 0.0 copy-start.2
  3.2 1.6 %copy-done.2 = bf16[128,8192]{1,0:T(8,128)(2,1)S(1)} copy-done((bf16[128,8192]{1,0:T(8,128)(2,1)S(1)}, bf16[128,8192]{1,0:T(8,128)(2,1)}, u32[]{:S(2)}) %copy-start.2) | copy-done | bytes 2097176
  4.8 0.0 copy-start.3
  4.8 0.8 %copy-done.3 = f32[32,256]{1,0:T(8,128)S(1)} copy-done((f32[32,256]{1,0:T(8,128)S(1)}, f32[32,256]{1,0:T(8,128)}, u32[]{:S(2)}) %copy-start.3) | copy-done | bytes 32792
  5.5 0.0 copy-start.4
  5.5 0.7 %copy-done.4 = f32[4096]{0:T(1024)S(1)} copy-done((f32[4096]{0:T(1024)S(1)}, f32[4096]{0:T(1024)}, u32[]{:S(2)}) %copy-start.4) | copy-done | bytes 16408
  6.3 0.0 copy-start.5
  6.3 0.7 copy-done.5
  6.9 58.6 %shard_map.64 = bf16[128,8192]{1,0:T(8,128)(2,1)S(1)} custom-call(s32[32]{0:T(128)S(1)} %copy-done.5, bf16[128,8192]{1,0:T(8,128)(2,1)S(1)} %copy-done, bf16[128,8192]{1,0:T(8,128)(2,1)S(1)} %copy-done.1, bf16[128,8192]{1,0:T(8,128)(2,1)S(1)} %copy-done.2, f32[32,256]{1,0:T(8,128)S(1)} %copy-done.3, f32[32,128]{1,0:T(8,128)S(1)} %bitcast.1), custom_call_target="tpu_custom_call" | custom-call | flops 1879048192 | bytes 8388608 | tf_op jit(solution)/shard_map/pallas_call | solution.py:446
  65.6 1.3 %copy.8 = bf16[128,8192]{1,0:T(8,128)(2,1)} copy(bf16[128,8192]{1,0:T(8,128)(2,1)S(1)} %shard_map.64) | data formatting | bytes 4194304
Async XLA Ops:
  0.0 1.6 %copy-start = (bf16[128,8192]{1,0:T(8,128)(2,1)S(1)}, bf16[128,8192]{1,0:T(8,128)(2,1)}, u32[]{:S(2)}) copy-start(bf16[128,8192]{1,0:T(8,128)(2,1)} %q_far.1) | copy-start | bytes 6291460
  1.6 1.6 %copy-start.1 = (bf16[128,8192]{1,0:T(8,128)(2,1)S(1)}, bf16[128,8192]{1,0:T(8,128)(2,1)}, u32[]{:S(2)}) copy-start(bf16[128,8192]{1,0:T(8,128)(2,1)} %k_far.1) | copy-start | bytes 6291460
  3.2 1.6 %copy-start.2 = (bf16[128,8192]{1,0:T(8,128)(2,1)S(1)}, bf16[128,8192]{1,0:T(8,128)(2,1)}, u32[]{:S(2)}) copy-start(bf16[128,8192]{1,0:T(8,128)(2,1)} %v_far.1) | copy-start | bytes 6291460
  4.8 0.8 %copy-start.3 = (f32[32,256]{1,0:T(8,128)S(1)}, f32[32,256]{1,0:T(8,128)}, u32[]{:S(2)}) copy-start(f32[32,256]{1,0:T(8,128)} %ld_ref.1) | copy-start | bytes 98308
  5.5 0.7 %copy-start.4 = (f32[4096]{0:T(1024)S(1)}, f32[4096]{0:T(1024)}, u32[]{:S(2)}) copy-start(f32[4096]{0:T(1024)} %param.11) | copy-start | bytes 49156
  6.3 0.7 copy-start.5

commit v4 on v3

--- a/solution.py
+++ b/solution.py
@@ -109,7 +109,7 @@
 
 MESH = pl.DeviceIdType.MESH
 GROUP = 8
-SUBS = 2
+SUBS = 4
 BATCH = 4
 TOP = 32766.0
 FAR_BELOW = -1e30
@@ -401,17 +401,21 @@
 
     loads[0].wait()
     loads[1].wait()
-    for sub in range(SUBS):
+    for sub in range(SUBS - 1):
         send_states(sub)
+    slab_totals(0)
+    send_states(SUBS - 1)
+    slab_totals(1)
     loads[2].wait()
-    slab_totals(0)
+    send_prefixes(0)
+    slab_totals(2)
+    send_prefixes(1)
     near_heads(0, 1)
-    send_prefixes(0)
-    near_heads(1, 3)
-    slab_totals(1)
-    near_heads(3, 4)
-    send_prefixes(1)
-    near_heads(4, GROUP)
+    slab_totals(3)
+    send_prefixes(2)
+    near_heads(1, 2)
+    send_prefixes(3)
+    near_heads(2, GROUP)
     for sub in range(SUBS):
         finish(me, sub, e_out.at[sub, me], em_out.at[sub, me])
 
@@ -457,7 +461,7 @@
             codes, codes, metas, metas, codes, codes, metas, metas, totals, totals,
         ] + [sems((SUBS, GROUP))] * 8 + [sems((SUBS,))] * 2 + [sems((2,))] * 2 + [sems((3,))],
         compiler_params=pltpu.CompilerParams(
-            collective_id=0, has_side_effects=True, vmem_limit_bytes=40 * 1024 * 1024
+            collective_id=0, has_side_effects=True, vmem_limit_bytes=58 * 1024 * 1024
         ),
         cost_estimate=pl.CostEstimate(
             flops=14 * count * rows * rows * width, bytes_accessed=8 * rows * columns,

time: 67.2 us -> 64.5 us (0.960)
  local copies, waits for them, and re-layouts: 8.22 us -> 3.1 us
  Pallas kernels: 58.6 us -> 61.1 us
    unnamed x13 -> x1, local copies, waits for them, and re-layouts: 8.22 us -> 3.1 us
    pallas_call x1, Pallas kernels: 58.6 us -> 61.1 us  [by_slabs(): pl.pallas_call(functools.partial(slab_kernel, slabs), out_shape=jax.Shape...]
where the time goes in v4:
time: 64.5 us; the launch traced here: 64.2 us
  Pallas kernels  61.1 us (95%)
  local copies, waits for them, and re-layouts  3.1 us (5%)
    pallas_call x1, Pallas kernels, by_slabs(): pl.pallas_call(functools.partial(slab_kernel, slabs), out_shape=jax.Shape...  61.1 us
    unnamed x1, local copies, waits for them, and re-layouts  3.1 us

profile of v4, /device:TPU:0, one launch (start us, length us, event | category | flops | bytes accessed | tf_op | source)
XLA Modules:
  0.0 64.2 jit_solution(9790030800073084920)
XLA Ops:
  0.0 61.1 %shard_map.64 = bf16[128,8192]{1,0:T(8,128)(2,1)} custom-call(s32[32]{0:T(128)} %doc_ref.1, bf16[128,8192]{1,0:T(8,128)(2,1)} %q_far.1, bf16[128,8192]{1,0:T(8,128)(2,1)} %k_far.1, bf16[128,8192]{1,0:T(8,128)(2,1)} %v_far.1, f32[32,256]{1,0:T(8,128)} %ld_ref.1, f32[32,128]{1,0:T(8,128)} %bitcast.1), custom_call_target="tpu_custom_call" | custom-call | flops 1879048192 | bytes 8388608 | tf_op jit(solution)/shard_map/pallas_call | solution.py:450
  61.1 3.1 %copy.8 = bf16[128,8192]{1,0:T(8,128)(2,1)} copy(bf16[128,8192]{1,0:T(8,128)(2,1)} %shard_map.64) | data formatting | bytes 4194304

commit v5 on v3

--- a/solution.py
+++ b/solution.py
@@ -112,6 +112,7 @@
 SUBS = 2
 BATCH = 4
 TOP = 32766.0
+NEAREST = 12582912.0
 FAR_BELOW = -1e30
 ORDER = (7, 6, 1, 5, 4, 3, 2)
 
@@ -138,7 +139,7 @@
 
 def to_code(state):
     scale = jnp.maximum(jnp.max(jnp.abs(state), axis=0, keepdims=True), 1e-30) * (1.0 / TOP)
-    code = jnp.round(state * (1.0 / scale)).astype(jnp.int32).astype(jnp.int16)
+    code = (state * (1.0 / scale) + NEAREST - NEAREST).astype(jnp.int32).astype(jnp.int16)
     return code, scale
 
 
@@ -149,7 +150,7 @@
 def slab_kernel(
     slabs,
     doc_ref, q_far, k_far, v_far, ld_ref, gain_ref, o_ref,
-    q_ref, k_ref, v_ref,
+    q_ref, k_ref, v_ref, keys_turned,
     ld_all, gain_all, cum_t, bias, near,
     s_out, s_in, sm_out, sm_in, e_out, e_in, em_out, em_in, t_out, t_in,
     s_ss, s_rs, sm_ss, sm_rs, e_ss, e_rs, em_ss, em_rs, t_ss, t_rs, x_ss, x_rs, l_s,
@@ -248,6 +249,7 @@
             cols = columns(g, c)
             high, low = halves(v_ref[:, cols].astype(jnp.float32) * tail[:, c:c + 1])
             key = jnp.transpose(k_ref[:, cols])
+            keys_turned[g * per_owner + c] = key
             states.append(jnp.dot(
                 jnp.concatenate([key, key], axis=1), jnp.concatenate([high, low], axis=0),
                 preferred_element_type=jnp.float32,
@@ -300,8 +302,8 @@
             for batch in range(0, per_owner, BATCH):
                 few = range(batch, batch + BATCH)
                 scores = [
-                    lax.dot_general(
-                        q_ref[:, columns(g, c)], k_ref[:, columns(g, c)], (((1,), (1,)), ((), ())),
+                    jnp.dot(
+                        q_ref[:, columns(g, c)], keys_turned[g * per_owner + c],
                         preferred_element_type=jnp.float32,
                     )
                     for c in few
@@ -405,13 +407,13 @@
         send_states(sub)
     loads[2].wait()
     slab_totals(0)
-    near_heads(0, 1)
+    near_heads(0, 2)
     send_prefixes(0)
-    near_heads(1, 3)
+    near_heads(2, 3)
     slab_totals(1)
-    near_heads(3, 4)
+    near_heads(3, 5)
     send_prefixes(1)
-    near_heads(4, GROUP)
+    near_heads(5, GROUP)
     for sub in range(SUBS):
         finish(me, sub, e_out.at[sub, me], em_out.at[sub, me])
 
@@ -449,6 +451,7 @@
         in_specs=[pl.BlockSpec(memory_space=pltpu.SMEM)] + [pl.BlockSpec(memory_space=pltpu.HBM)] * 3 + [vmem] * 2,
         out_specs=vmem,
         scratch_shapes=[pltpu.VMEM((rows, columns), jnp.bfloat16)] * 3 + [
+            pltpu.VMEM((count, width, rows), jnp.bfloat16),
             pltpu.VMEM((count, rows), jnp.float32),
             pltpu.VMEM((count, width), jnp.float32),
             pltpu.VMEM((GROUP, rows, count // GROUP), jnp.float32),
@@ -457,7 +460,7 @@
             codes, codes, metas, metas, codes, codes, metas, metas, totals, totals,
         ] + [sems((SUBS, GROUP))] * 8 + [sems((SUBS,))] * 2 + [sems((2,))] * 2 + [sems((3,))],
         compiler_params=pltpu.CompilerParams(
-            collective_id=0, has_side_effects=True, vmem_limit_bytes=40 * 1024 * 1024
+            collective_id=0, has_side_effects=True, vmem_limit_bytes=58 * 1024 * 1024
         ),
         cost_estimate=pl.CostEstimate(
             flops=14 * count * rows * rows * width, bytes_accessed=8 * rows * columns,

time: 67.2 us -> 63.2 us (0.940)
  local copies, waits for them, and re-layouts: 8.22 us -> 3.1 us
  Pallas kernels: 58.6 us -> 59.8 us
    unnamed x13 -> x1, local copies, waits for them, and re-layouts: 8.22 us -> 3.1 us
    pallas_call x1, Pallas kernels: 58.6 us -> 59.8 us  [by_slabs(): pl.pallas_call(functools.partial(slab_kernel, slabs), out_shape=jax.Shape...]
where the time goes in v5:
time: 63.2 us; the launch traced here: 62.9 us
  Pallas kernels  59.8 us (95%)
  local copies, waits for them, and re-layouts  3.1 us (5%)
    pallas_call x1, Pallas kernels, by_slabs(): pl.pallas_call(functools.partial(slab_kernel, slabs), out_shape=jax.Shape...  59.8 us
    unnamed x1, local copies, waits for them, and re-layouts  3.1 us

profile of v5, /device:TPU:0, one launch (start us, length us, event | category | flops | bytes accessed | tf_op | source)
XLA Modules:
  0.0 62.9 jit_solution(16306286839121212542)
XLA Ops:
  0.0 59.8 %shard_map.64 = bf16[128,8192]{1,0:T(8,128)(2,1)} custom-call(s32[32]{0:T(128)} %doc_ref.1, bf16[128,8192]{1,0:T(8,128)(2,1)} %q_far.1, bf16[128,8192]{1,0:T(8,128)(2,1)} %k_far.1, bf16[128,8192]{1,0:T(8,128)(2,1)} %v_far.1, f32[32,256]{1,0:T(8,128)} %ld_ref.1, f32[32,128]{1,0:T(8,128)} %bitcast.1), custom_call_target="tpu_custom_call" | custom-call | flops 1879048192 | bytes 8388608 | tf_op jit(solution)/shard_map/pallas_call | solution.py:448
  59.8 3.1 %copy.8 = bf16[128,8192]{1,0:T(8,128)(2,1)} copy(bf16[128,8192]{1,0:T(8,128)(2,1)} %shard_map.64) | data formatting | bytes 4194304

commit v6 on v5

--- a/solution.py
+++ b/solution.py
@@ -460,7 +460,7 @@
             codes, codes, metas, metas, codes, codes, metas, metas, totals, totals,
         ] + [sems((SUBS, GROUP))] * 8 + [sems((SUBS,))] * 2 + [sems((2,))] * 2 + [sems((3,))],
         compiler_params=pltpu.CompilerParams(
-            collective_id=0, has_side_effects=True, vmem_limit_bytes=58 * 1024 * 1024
+            collective_id=0, has_side_effects=True, vmem_limit_bytes=50 * 1024 * 1024
         ),
         cost_estimate=pl.CostEstimate(
             flops=14 * count * rows * rows * width, bytes_accessed=8 * rows * columns,

time: 63.2 us -> 62 us (0.981)
  Pallas kernels: 59.8 us -> 58.2 us
    pallas_call x1, Pallas kernels: 59.8 us -> 58.2 us  [by_slabs(): pl.pallas_call(functools.partial(slab_kernel, slabs), out_shape=jax.Shape...]
    unnamed x1 -> x7, local copies, waits for them, and re-layouts: 3.1 us -> 3.45 us
where the time goes in v6:
time: 62 us; the launch traced here: 61.7 us
  Pallas kernels  58.2 us (94%)
  local copies, waits for them, and re-layouts  3.45 us (6%)
    pallas_call x1, Pallas kernels, by_slabs(): pl.pallas_call(functools.partial(slab_kernel, slabs), out_shape=jax.Shape...  58.2 us
    unnamed x7, local copies, waits for them, and re-layouts  3.45 us

profile of v6, /device:TPU:0, one launch (start us, length us, event | category | flops | bytes accessed | tf_op | source)
XLA Modules:
  0.0 61.7 jit_solution(5631980135418325211)
XLA Ops:
  0.0 0.0 copy-start
  0.0 0.8 %copy-done = f32[32,256]{1,0:T(8,128)S(1)} copy-done((f32[32,256]{1,0:T(8,128)S(1)}, f32[32,256]{1,0:T(8,128)}, u32[]{:S(2)}) %copy-start) | copy-done | bytes 32792
  0.8 0.0 copy-start.1
  0.8 0.7 %copy-done.1 = f32[4096]{0:T(1024)S(1)} copy-done((f32[4096]{0:T(1024)S(1)}, f32[4096]{0:T(1024)}, u32[]{:S(2)}) %copy-start.1) | copy-done | bytes 16408
  1.5 0.0 copy-start.2
  1.5 0.7 %copy-done.2 = s32[32]{0:T(128)S(1)} copy-done((s32[32]{0:T(128)S(1)}, s32[32]{0:T(128)}, u32[]{:S(2)}) %copy-start.2) | copy-done | bytes 152
  2.1 58.2 %shard_map.64 = bf16[128,8192]{1,0:T(8,128)(2,1)S(1)} custom-call(s32[32]{0:T(128)S(1)} %copy-done.2, bf16[128,8192]{1,0:T(8,128)(2,1)} %q_far.1, bf16[128,8192]{1,0:T(8,128)(2,1)} %k_far.1, bf16[128,8192]{1,0:T(8,128)(2,1)} %v_far.1, f32[32,256]{1,0:T(8,128)S(1)} %copy-done, f32[32,128]{1,0:T(8,128)S(1)} %bitcast.1), custom_call_target="tpu_custom_call" | custom-call | flops 1879048192 | bytes 8388608 | tf_op jit(solution)/shard_map/pallas_call | solution.py:448
  60.4 1.3 %copy.8 = bf16[128,8192]{1,0:T(8,128)(2,1)} copy(bf16[128,8192]{1,0:T(8,128)(2,1)S(1)} %shard_map.64) | data formatting | bytes 4194304
Async XLA Ops:
  0.0 0.8 %copy-start = (f32[32,256]{1,0:T(8,128)S(1)}, f32[32,256]{1,0:T(8,128)}, u32[]{:S(2)}) copy-start(f32[32,256]{1,0:T(8,128)} %ld_ref.1) | copy-start | bytes 98308
  0.8 0.7 %copy-start.1 = (f32[4096]{0:T(1024)S(1)}, f32[4096]{0:T(1024)}, u32[]{:S(2)}) copy-start(f32[4096]{0:T(1024)} %param.11) | copy-start | bytes 49156
  1.5 0.7 %copy-start.2 = (s32[32]{0:T(128)S(1)}, s32[32]{0:T(128)}, u32[]{:S(2)}) copy-start(s32[32]{0:T(128)} %doc_ref.1) | copy-start | bytes 388

commit v7 on v6

--- a/solution.py
+++ b/solution.py
@@ -202,8 +202,13 @@
     ]
     for swap in swaps:
         swap.start()
-    ld_all[mine, :] = ld_ref[:, pl.ds(pl.multiple_of(half * rows, rows), rows)]
-    gain_all[mine, :] = gain_ref[...]
+    keeps = [
+        pltpu.make_async_copy(
+            ld_ref.at[:, pl.ds(pl.multiple_of(half * rows, rows), rows)], ld_all.at[mine], l_s.at[3]),
+        pltpu.make_async_copy(gain_ref, gain_all.at[mine], l_s.at[4]),
+    ]
+    for keep in keeps:
+        keep.start()
 
     first = block * rows
     down = lax.broadcasted_iota(jnp.int32, (rows, rows), 0)
@@ -225,8 +230,8 @@
     in_prior = (doc_few == prior).astype(jnp.float32)
     passes = (jnp.full((1, per_owner), final, jnp.int32) == prior).astype(jnp.float32)
 
-    for swap in swaps:
-        swap.wait()
+    for copy in keeps + swaps:
+        copy.wait()
     cum = jnp.dot(
         ld_all[...], (down <= along).astype(jnp.float32),
         precision=HIGHEST, preferred_element_type=jnp.float32,
@@ -448,7 +453,7 @@
     return pl.pallas_call(
         functools.partial(slab_kernel, slabs),
         out_shape=jax.ShapeDtypeStruct((rows, columns), jnp.bfloat16),
-        in_specs=[pl.BlockSpec(memory_space=pltpu.SMEM)] + [pl.BlockSpec(memory_space=pltpu.HBM)] * 3 + [vmem] * 2,
+        in_specs=[pl.BlockSpec(memory_space=pltpu.SMEM)] + [pl.BlockSpec(memory_space=pltpu.HBM)] * 5,
         out_specs=vmem,
         scratch_shapes=[pltpu.VMEM((rows, columns), jnp.bfloat16)] * 3 + [
             pltpu.VMEM((count, width, rows), jnp.bfloat16),
@@ -458,7 +463,7 @@
             pltpu.VMEM((rows, rows), jnp.float32),
             pltpu.VMEM((rows, columns), jnp.float32),
             codes, codes, metas, metas, codes, codes, metas, metas, totals, totals,
-        ] + [sems((SUBS, GROUP))] * 8 + [sems((SUBS,))] * 2 + [sems((2,))] * 2 + [sems((3,))],
+        ] + [sems((SUBS, GROUP))] * 8 + [sems((SUBS,))] * 2 + [sems((2,))] * 2 + [sems((5,))],
         compiler_params=pltpu.CompilerParams(
             collective_id=0, has_side_effects=True, vmem_limit_bytes=50 * 1024 * 1024
         ),

time: 62 us -> 62 us (level)
  no operation moved by 1% of the time
where the time goes in v7:
time: 62 us; the launch traced here: 61.7 us
  Pallas kernels  58.2 us (94%)
  local copies, waits for them, and re-layouts  3.45 us (6%)
    pallas_call x1, Pallas kernels, by_slabs(): pl.pallas_call(functools.partial(slab_kernel, slabs), out_shape=jax.Shape...  58.2 us
    unnamed x7, local copies, waits for them, and re-layouts  3.45 us

profile of v7, /device:TPU:0, one launch (start us, length us, event | category | flops | bytes accessed | tf_op | source)
XLA Modules:
  0.0 61.7 jit_solution(2062151900079777049)
XLA Ops:
  0.0 0.0 copy-start
  0.0 0.8 %copy-done = f32[32,256]{1,0:T(8,128)S(1)} copy-done((f32[32,256]{1,0:T(8,128)S(1)}, f32[32,256]{1,0:T(8,128)}, u32[]{:S(2)}) %copy-start) | copy-done | bytes 32792
  0.8 0.0 copy-start.1
  0.8 0.7 %copy-done.1 = f32[4096]{0:T(1024)S(1)} copy-done((f32[4096]{0:T(1024)S(1)}, f32[4096]{0:T(1024)}, u32[]{:S(2)}) %copy-start.1) | copy-done | bytes 16408
  1.5 0.0 copy-start.2
  1.5 0.7 %copy-done.2 = s32[32]{0:T(128)S(1)} copy-done((s32[32]{0:T(128)S(1)}, s32[32]{0:T(128)}, u32[]{:S(2)}) %copy-start.2) | copy-done | bytes 152
  2.1 58.2 %shard_map.64 = bf16[128,8192]{1,0:T(8,128)(2,1)S(1)} custom-call(s32[32]{0:T(128)S(1)} %copy-done.2, bf16[128,8192]{1,0:T(8,128)(2,1)} %q_far.1, bf16[128,8192]{1,0:T(8,128)(2,1)} %k_far.1, bf16[128,8192]{1,0:T(8,128)(2,1)} %v_far.1, f32[32,256]{1,0:T(8,128)S(1)} %copy-done, f32[32,128]{1,0:T(8,128)S(1)} %bitcast.1), custom_call_target="tpu_custom_call" | custom-call | flops 1879048192 | bytes 8388608 | tf_op jit(solution)/shard_map/pallas_call | solution.py:453
  60.4 1.3 %copy.8 = bf16[128,8192]{1,0:T(8,128)(2,1)} copy(bf16[128,8192]{1,0:T(8,128)(2,1)S(1)} %shard_map.64) | data formatting | bytes 4194304
Async XLA Ops:
  0.0 0.8 %copy-start = (f32[32,256]{1,0:T(8,128)S(1)}, f32[32,256]{1,0:T(8,128)}, u32[]{:S(2)}) copy-start(f32[32,256]{1,0:T(8,128)} %ld_ref.1) | copy-start | bytes 98308
  0.8 0.7 %copy-start.1 = (f32[4096]{0:T(1024)S(1)}, f32[4096]{0:T(1024)}, u32[]{:S(2)}) copy-start(f32[4096]{0:T(1024)} %param.11) | copy-start | bytes 49156
  1.5 0.7 %copy-start.2 = (s32[32]{0:T(128)S(1)}, s32[32]{0:T(128)}, u32[]{:S(2)}) copy-start(s32[32]{0:T(128)} %doc_ref.1) | copy-start | bytes 388
